TPU v7x, 32 devices: a whole 2x2x4 slice. The times are simulated.
32 devices in a mesh: dp: 8 (over z, y), expert: 4 (over x, core).
Axes of the slice: x: 2, y: 2, z: 4, core: 2. Of those that a mesh axis runs over, the one named last changes fastest.
Arguments:
- tokens: bfloat16 [1024, 4096], P('dp', 'expert'), may hold values from -24 to 24
- expert_ids: int32 [1024, 8], P('dp'), may hold values from 0 to 63, all different within a row; in each aligned block of 128 rows (0 to 127, 128 to 255, ...) at most 20 rows name the same one
- route_weights: float32 [1024, 8], P('dp'), may hold values from 0.05 to 1
- gate_weight: bfloat16 [64, 1536, 4096], P('dp', 'expert'), may hold values from -0.09375 to 0.09375
- up_weight: bfloat16 [64, 1536, 4096], P('dp', 'expert'), may hold values from -0.09375 to 0.09375
- down_weight: bfloat16 [64, 1536, 4096], P('dp', None, 'expert'), may hold values from -0.15625 to 0.15625
Outputs:
- quant_out: bfloat16 [1024, 4096], P('dp', 'expert')
- float_out: float32 [1024, 4096], P('dp', 'expert')
Inputs may be any that keep to these rules, and one draw needn't show every extreme that they name: `expert_ids`: each row names 8 different experts; every expert is named by some row; within the 128 rows of one index of dp no expert is named more than 20 times, and in every draw some expert is named exactly 20 times in some such block.
All inputs are finite; a program needn't handle non-finite values. Where the computation divides by a largest or mean magnitude, that divisor is 1e-20 or more.
Results may differ from a plain program's by a relative error of at most 0.011.
Values may be sent and summed in bfloat16 or wider, within the bound.
No kernel may reach another device: no remote copies, remote signals or barrier semaphores. Data moves between devices by JAX's collectives and lax.ppermute only.
A program may use at most 192 MiB of HBM per device.

v0:
```python
import functools

import jax
import jax.numpy as jnp
from jax import lax
from jax.experimental import pallas as pl
from jax.experimental.pallas import tpu as pltpu
from jax.sharding import PartitionSpec as P

CAP = 20
UNIT = 4
LEVELS = 7.0
EPS = 1e-06
VMEM = 56 * 1024 * 1024
LANES = 128
SLAB = 16
CHUNK = 1024
BRIEF = pl.CostEstimate(flops=1, bytes_accessed=1, transcendentals=0)

FRACTION_BF16 = (6.55787162, -12.52307356, 9.17209913)

bf16 = jnp.bfloat16
f32 = jnp.float32


def fraction(r, coefficients):
    dtype = r.dtype
    square = r * r
    total = jnp.asarray(coefficients[-1], dtype)
    for c in coefficients[-2::-1]:
        total = total * square + jnp.asarray(c, dtype)
    return (r * square) * total


def level_bf16(v):
    n = jnp.round(v)
    r = (v - n).astype(bf16)
    return n.astype(bf16) + fraction(r, FRACTION_BF16)


def level_mixed(v):
    n = jnp.round(v)
    return n + fraction((v - n).astype(bf16), FRACTION_BF16).astype(f32)


def fold_max(x):
    if x.shape[1] % LANES:
        return jnp.max(x, axis=1, keepdims=True)
    out = x[:, :LANES]
    for c in range(LANES, x.shape[1], LANES):
        out = jnp.maximum(out, x[:, c : c + LANES])
    return out


def wide(x, width):
    return jnp.concatenate([x] * (width // LANES), axis=1)


def dot_t(a, b):
    return lax.dot_general(a, b, (((1,), (1,)), ((), ())), preferred_element_type=f32)


def flipped(x):
    high, broad = -x.shape[0] % LANES, -x.shape[1] % LANES
    return jnp.pad(x, ((0, high), (0, broad))).T[: x.shape[1], : x.shape[0]]


def params():
    return pltpu.CompilerParams(vmem_limit_bytes=VMEM)


def prep_kernel(local_experts, groups, choices, first_ref, route_ref, hot_ref, share_ref):
    units = groups // UNIT
    group_tokens = route_ref.shape[1]
    unit_rows, unit_tokens = UNIT * CAP, UNIT * group_tokens
    first = first_ref[0].astype(f32)
    before = lax.broadcasted_iota(jnp.int32, (group_tokens, group_tokens), 0) < lax.broadcasted_iota(
        jnp.int32, (group_tokens, group_tokens), 1
    )
    before = jnp.where(before, 1.0, 0.0).astype(bf16)
    codes, weights = [], []
    for g in range(groups):
        base = 2 * choices * g
        ids = route_ref[base : base + choices, :]
        route = route_ref[base + choices : base + 2 * choices, :]
        shares = route / jnp.sum(route, axis=0, keepdims=True)
        hits, mine = [], []
        for e in range(local_experts):
            hit = ids == first + float(e)
            hits.append(jnp.max(jnp.where(hit, 1.0, 0.0), axis=0, keepdims=True))
            mine.append(jnp.sum(jnp.where(hit, shares, 0.0), axis=0, keepdims=True))
        part = jnp.concatenate(hits, axis=0)
        weights.append(jnp.concatenate(mine, axis=0))
        slot = jnp.dot(part.astype(bf16), before, preferred_element_type=f32)
        codes.append(jnp.where(part > 0.5, slot + float((g % UNIT) * CAP), -1.0))
    row = lax.broadcasted_iota(jnp.int32, (unit_rows, unit_tokens), 0).astype(f32)
    for u in range(units):
        code = jnp.concatenate(codes[u * UNIT : (u + 1) * UNIT], axis=1)
        weight = jnp.concatenate(weights[u * UNIT : (u + 1) * UNIT], axis=1)
        for e in range(local_experts):
            hot = row == code[e : e + 1, :]
            hot_ref[u, e * unit_rows : (e + 1) * unit_rows, :] = jnp.where(hot, 1.0, 0.0).astype(bf16)
            share_ref[e, u * unit_rows : (u + 1) * unit_rows, :] = jnp.sum(
                jnp.where(hot, weight[e : e + 1, :], 0.0), axis=1, keepdims=True
            )


def prep(first, route, local_experts, groups, choices):
    units = groups // UNIT
    return pl.pallas_call(
        functools.partial(prep_kernel, local_experts, groups, choices),
        out_shape=(
            jax.ShapeDtypeStruct((units, local_experts * UNIT * CAP, UNIT * route.shape[1]), bf16),
            jax.ShapeDtypeStruct((local_experts, groups * CAP, 1), f32),
        ),
        in_specs=[
            pl.BlockSpec(memory_space=pltpu.SMEM),
            pl.BlockSpec(memory_space=pltpu.VMEM),
        ],
        out_specs=(pl.BlockSpec(memory_space=pltpu.VMEM), pl.BlockSpec(memory_space=pltpu.VMEM)),
        compiler_params=params(),
        name="routing_tables",
    )(first, route)


def channel_peak_kernel(gate_ref, up_ref, peak_ref):
    hidden, depth = gate_ref.shape[1:]

    def one(i, carry):
        cols = pl.ds(pl.multiple_of(i * CHUNK, CHUNK), CHUNK)
        top = None
        for ref in (gate_ref, up_ref):
            for f in range(0, hidden, SLAB):
                value = jnp.abs(ref[0, f : f + SLAB, cols])
                top = value if top is None else jnp.maximum(top, value)
        peak_ref[0, :, cols] = jnp.max(top.astype(f32), axis=0, keepdims=True)
        return carry

    lax.fori_loop(0, depth // CHUNK, one, 0)


def channel_peak(gate, up):
    experts, hidden, depth = gate.shape
    spec = pl.BlockSpec((1, hidden, depth), lambda e: (e, 0, 0))
    return pl.pallas_call(
        channel_peak_kernel,
        grid=(experts,),
        out_shape=jax.ShapeDtypeStruct((experts, 1, depth), f32),
        in_specs=[spec, spec],
        out_specs=pl.BlockSpec((1, 1, depth), lambda e: (e, 0, 0)),
        compiler_params=params(),
        cost_estimate=BRIEF,
        name="channel_peak",
    )(gate, up)


def down_quant_kernel(rows, width, down_ref, level_ref, scale_ref):
    step = 8 * SLAB

    def peak(i, carry):
        base = pl.multiple_of(i * step, step)
        for j in range(0, step, SLAB):
            carry = jnp.maximum(carry, jnp.abs(down_ref[0, pl.ds(base + j, SLAB), :]))
        return carry

    top = lax.fori_loop(0, rows // step, peak, jnp.zeros((SLAB, width), bf16))
    top = jnp.max(top.astype(f32), axis=0, keepdims=True) + EPS
    scale_ref[0] = top / LEVELS
    inverse = jnp.broadcast_to(LEVELS / top, (SLAB, width))

    def quantize(i, carry):
        base = pl.multiple_of(i * step, step)
        for j in range(0, step, SLAB):
            value = down_ref[0, pl.ds(base + j, SLAB), :].astype(f32) * inverse
            level_ref[0, pl.ds(base + j, SLAB), :] = level_bf16(value)
        return carry

    lax.fori_loop(0, rows // step, quantize, 0)


def down_quant(down):
    experts, hidden, width = down.shape
    block = 512
    return pl.pallas_call(
        functools.partial(down_quant_kernel, hidden, block),
        grid=(experts, width // block),
        out_shape=(
            jax.ShapeDtypeStruct(down.shape, bf16),
            jax.ShapeDtypeStruct((experts, 1, width), f32),
        ),
        in_specs=[pl.BlockSpec((1, hidden, block), lambda e, c: (e, 0, c))],
        out_specs=(
            pl.BlockSpec((1, hidden, block), lambda e, c: (e, 0, c)),
            pl.BlockSpec((1, 1, block), lambda e, c: (e, 0, c)),
        ),
        compiler_params=params(),
        cost_estimate=BRIEF,
        name="down_levels",
    )(down)


def rows_kernel(local_experts, units, hot_ref, tokens_ref, peak_ref, rows_ref, smooth_ref):
    unit_rows = UNIT * CAP
    group_tokens, width = tokens_ref.shape[2], tokens_ref.shape[3]
    top = [None] * local_experts
    for u in range(units):
        tokens = tokens_ref[u * UNIT : (u + 1) * UNIT, 0].reshape(UNIT * group_tokens, width)
        picked = jnp.dot(hot_ref[u], tokens, preferred_element_type=f32)
        for e in range(local_experts):
            part = picked[e * unit_rows : (e + 1) * unit_rows]
            rows_ref[e, u * unit_rows : (u + 1) * unit_rows, :] = part.astype(bf16)
            most = jnp.max(jnp.abs(part), axis=0, keepdims=True)
            top[e] = most if top[e] is None else jnp.maximum(top[e], most)
    for e in range(local_experts):
        smooth_ref[e] = jnp.sqrt(jnp.maximum(top[e], 1.0) / (peak_ref[e : e + 1, :] + EPS))


def expert_rows(hot, tokens, weight_peak, local_experts, groups):
    shards, group_tokens, share = tokens.shape[1:]
    units = groups // UNIT
    block = 512
    per = share // block
    return pl.pallas_call(
        functools.partial(rows_kernel, local_experts, units),
        grid=(shards * per,),
        out_shape=(
            jax.ShapeDtypeStruct((local_experts, groups * CAP, shards * share), bf16),
            jax.ShapeDtypeStruct((local_experts, 1, shards * share), f32),
        ),
        in_specs=[
            pl.BlockSpec(hot.shape, lambda c: (0, 0, 0)),
            pl.BlockSpec((groups, 1, group_tokens, block), lambda c: (0, c // per, 0, c % per)),
            pl.BlockSpec((local_experts, block), lambda c: (0, c)),
        ],
        out_specs=(
            pl.BlockSpec((local_experts, groups * CAP, block), lambda c: (0, 0, c)),
            pl.BlockSpec((local_experts, 1, block), lambda c: (0, 0, c)),
        ),
        compiler_params=params(),
        name="expert_rows",
    )(hot, tokens, weight_peak)


def silu_product(both):
    half = both.shape[0] // 2
    gate, up = both[:half], both[half:]
    return flipped(gate / (1.0 + jnp.exp(-gate)) * up).astype(bf16)


def float_kernel(
    rows_ref, gate_ref, up_ref, smooth_ref,
    hidden_ref, inverse_w, scale_w, inverse_r, scale_r,
    smooth_s, unsmooth_s, top_s, top_r, acc,
):
    count = rows_ref.shape[1]
    hidden = gate_ref.shape[1]
    chunks = gate_ref.shape[2] // CHUNK
    weights = ((gate_ref, 0), (up_ref, hidden))

    smooth = smooth_ref[0]
    smooth_s[...] = jnp.broadcast_to(smooth, smooth_s.shape)
    unsmooth_s[...] = jnp.broadcast_to(1.0 / smooth, unsmooth_s.shape)
    top_s[...] = jnp.zeros_like(top_s)
    top_r[...] = jnp.zeros_like(top_r)
    acc[...] = jnp.zeros_like(acc)

    def peaks(i, carry):
        cols = pl.ds(pl.multiple_of(i * CHUNK, CHUNK), CHUNK)
        smooth_c = smooth_s[:, cols]
        unsmooth_c = unsmooth_s[:, cols]
        rows = rows_ref[0, :, cols]
        for ref, base in weights:
            acc[base : base + hidden, :] += dot_t(ref[0, :, cols], rows)
            for f in range(0, hidden, SLAB):
                value = jnp.abs(ref[0, f : f + SLAB, cols]).astype(f32) * smooth_c
                spot = slice(base + f, base + f + SLAB)
                top_s[spot, :] = jnp.maximum(top_s[spot, :], fold_max(value))
        for r in range(0, count, SLAB):
            value = jnp.abs(rows_ref[0, r : r + SLAB, cols]).astype(f32) * unsmooth_c
            top_r[r : r + SLAB, :] = jnp.maximum(top_r[r : r + SLAB, :], fold_max(value))
        return carry

    lax.fori_loop(0, chunks, peaks, 0)
    hidden_ref[0] = silu_product(acc[...])

    for r in range(0, count, SLAB):
        top = jnp.max(top_r[r : r + SLAB, :], axis=1, keepdims=True) + EPS
        inverse_r[0, r : r + SLAB, :] = jnp.broadcast_to(LEVELS / top, (SLAB, LANES))
        scale_r[0, r : r + SLAB, :] = jnp.broadcast_to(top / LEVELS, (SLAB, LANES))
    for f in range(0, 2 * hidden, LANES):
        top = jnp.max(top_s[f : f + LANES, :], axis=1, keepdims=True) + EPS
        inverse_w[0, f : f + LANES, :] = jnp.broadcast_to(LEVELS / top, (LANES, LANES))
        scale_w[0, f : f + LANES, :] = jnp.broadcast_to(top / LEVELS, (LANES, LANES))


def float_hidden(rows, gate, up, smooth):
    experts, count, depth = rows.shape
    hidden = gate.shape[1]

    def spec(*tail):
        return pl.BlockSpec((1,) + tail, lambda e: (e,) + (0,) * len(tail))

    tails = ((count, hidden), (2 * hidden, LANES), (2 * hidden, LANES), (count, LANES), (count, LANES))
    kinds = (bf16, f32, f32, f32, f32)
    return pl.pallas_call(
        float_kernel,
        grid=(experts,),
        out_shape=tuple(jax.ShapeDtypeStruct((experts,) + s, k) for s, k in zip(tails, kinds)),
        in_specs=[spec(count, depth), spec(hidden, depth), spec(hidden, depth), spec(1, depth)],
        out_specs=tuple(spec(*s) for s in tails),
        scratch_shapes=[
            pltpu.VMEM((SLAB, depth), f32),
            pltpu.VMEM((SLAB, depth), f32),
            pltpu.VMEM((2 * hidden, LANES), f32),
            pltpu.VMEM((count, LANES), f32),
            pltpu.VMEM((2 * hidden, count), f32),
        ],
        compiler_params=params(),
        cost_estimate=BRIEF,
        name="float_hidden",
    )(rows, gate, up, smooth)


def quant_kernel(
    rows_ref, gate_ref, up_ref, smooth_ref, inverse_w, scale_w, inverse_r, scale_r, *refs
):
    hidden_ref, smooth_s, unsmooth_s, acc, levels, row_levels = refs[-6:]
    count = rows_ref.shape[1]
    hidden = gate_ref.shape[1]
    chunks = gate_ref.shape[2] // CHUNK
    weights = ((gate_ref, 0), (up_ref, hidden))

    smooth = smooth_ref[0]
    smooth_s[...] = jnp.broadcast_to(smooth, smooth_s.shape)
    unsmooth_s[...] = jnp.broadcast_to(1.0 / smooth, unsmooth_s.shape)
    acc[...] = jnp.zeros_like(acc)

    def quantize(i, slot):
        cols = pl.ds(pl.multiple_of(i * CHUNK, CHUNK), CHUNK)
        smooth_c = smooth_s[:, cols]
        unsmooth_c = unsmooth_s[:, cols]
        for r in range(0, count, SLAB):
            value = rows_ref[0, r : r + SLAB, cols].astype(f32) * unsmooth_c
            value = value * wide(inverse_r[0, r : r + SLAB, :], CHUNK)
            level = level_mixed(value) * wide(scale_r[0, r : r + SLAB, :], CHUNK)
            row_levels[slot, r : r + SLAB, :] = level.astype(bf16)
        for ref, base in weights:
            for f in range(0, hidden, SLAB):
                value = ref[0, f : f + SLAB, cols].astype(f32) * smooth_c
                value = value * wide(inverse_w[0, base + f : base + f + SLAB, :], CHUNK)
                levels[slot, base + f : base + f + SLAB, :] = level_bf16(value)

    def multiply(slot):
        acc[...] += dot_t(levels[slot], row_levels[slot])

    quantize(0, 0)

    def pair(i, carry):
        multiply(0)
        quantize(2 * i + 1, 1)
        multiply(1)
        quantize(2 * i + 2, 0)
        return carry

    lax.fori_loop(0, chunks // 2 - 1, pair, 0)
    multiply(0)
    quantize(chunks - 1, 1)
    multiply(1)

    hidden_ref[0] = silu_product(acc[...] * scale_w[0][:, :1])


def quant_hidden(rows, gate, up, smooth, scales, first, amount, space, at, into=None):
    count, depth = rows.shape[1:]
    hidden = gate.shape[1]
    extra = [] if into is None else [into]

    def spec(*tail):
        return pl.BlockSpec((1,) + tail, lambda e: (first + e,) + (0,) * len(tail))

    return pl.pallas_call(
        quant_kernel,
        grid=(amount,),
        out_shape=jax.ShapeDtypeStruct((space, count, hidden), bf16),
        in_specs=[spec(*a.shape[1:]) for a in (rows, gate, up, smooth) + scales]
        + [pl.BlockSpec(memory_space=pl.ANY)] * len(extra),
        out_specs=pl.BlockSpec((1, count, hidden), lambda e: (at + e, 0, 0)),
        input_output_aliases={8: 0} if extra else {},
        scratch_shapes=[
            pltpu.VMEM((SLAB, depth), f32),
            pltpu.VMEM((SLAB, depth), f32),
            pltpu.VMEM((2 * hidden, count), f32),
            pltpu.VMEM((2, 2 * hidden, CHUNK), bf16),
            pltpu.VMEM((2, count, CHUNK), bf16),
        ],
        compiler_params=params(),
        cost_estimate=BRIEF,
        name="quant_hidden",
    )(rows, gate, up, smooth, *scales, *extra)


def combine_kernel(quantized, skip, last, *refs):
    share_ref, hidden_ref, down_ref, scale_ref = refs[:4]
    e = pl.program_id(0)
    shards, _, count, part = hidden_ref.shape
    unit_rows = UNIT * CAP
    wide_s = refs[-1]
    for r in range(0, count, SLAB):
        spot = slice(r, r + SLAB)
        if not quantized:
            for s in range(shards):
                wide_s[spot, s * part : (s + 1) * part] = hidden_ref[s, 0, spot, :]
            continue
        top = None
        for s in range(shards):
            value = fold_max(jnp.abs(hidden_ref[s, 0, spot, :]).astype(f32))
            top = value if top is None else jnp.maximum(top, value)
        top = jnp.max(top, axis=1, keepdims=True) + EPS
        inverse, scale = LEVELS / top, top / LEVELS
        for s in range(shards):
            value = level_mixed(hidden_ref[s, 0, spot, :].astype(f32) * inverse) * scale
            wide_s[spot, s * part : (s + 1) * part] = value.astype(bf16)

    out = jnp.dot(wide_s[...], down_ref[0], preferred_element_type=f32) * scale_ref[0] * share_ref[0]
    out = out.astype(bf16)
    units = count // unit_rows
    if not last:
        for u in range(units):
            refs[-2][u] = out[u * unit_rows : (u + 1) * unit_rows]
        return
    hot_ref, out_ref, keep_s = refs[4], refs[-3], refs[-2]
    if skip:

        @pl.when(e == 0)
        def _():
            keep_s[:, : skip * unit_rows, :] = refs[5][...]

    at = pl.ds(pl.multiple_of((skip + e) * unit_rows, SLAB), unit_rows)
    for u in range(units):
        keep_s[u, at, :] = out[u * unit_rows : (u + 1) * unit_rows]

    @pl.when(e == pl.num_programs(0) - 1)
    def _():
        tokens = hot_ref.shape[1]
        for u in range(units):
            out_ref[u * tokens : (u + 1) * tokens, :] = jnp.dot(
                hot_ref[u], keep_s[u], preferred_element_type=f32
            ).astype(bf16)


def combine(hot_t, share, hidden, down, scale, quantized, first=0, at=0, pieces=1, last=True, earlier=None):
    units, unit_tokens, hot_rows = hot_t.shape
    shards, amount, count, part = hidden.shape
    units_hidden, width = down.shape[1:]
    block = width // pieces
    unit_rows = UNIT * CAP
    in_specs = [
        pl.BlockSpec((1, count, 1), lambda e: (first + e, 0, 0)),
        pl.BlockSpec((shards, 1, count, part), lambda e: (0, e, 0, 0)),
        pl.BlockSpec((1, units_hidden, block), lambda e: (first + e, 0, at)),
        pl.BlockSpec((1, 1, block), lambda e: (first + e, 0, at)),
    ]
    operands = [share, hidden, down, scale]
    scratch = [pltpu.VMEM((count, units_hidden), bf16)]
    if last:
        operands.append(hot_t)
        in_specs.append(pl.BlockSpec(hot_t.shape, lambda e: (0, 0, 0)))
        scratch = [pltpu.VMEM((units, hot_rows, block), bf16)] + scratch
        out_shape = jax.ShapeDtypeStruct((units * unit_tokens, block), bf16)
        out_spec = pl.BlockSpec((units * unit_tokens, block), lambda e: (0, 0))
        if first:
            operands.append(earlier)
            in_specs.append(pl.BlockSpec((units, first * unit_rows, block), lambda e: (0, 0, at)))
    else:
        out_shape = jax.ShapeDtypeStruct((units, amount * unit_rows, block), bf16)
        out_spec = pl.BlockSpec((units, unit_rows, block), lambda e: (0, e, 0))
    return pl.pallas_call(
        functools.partial(combine_kernel, quantized, first, last),
        grid=(amount,),
        out_shape=out_shape,
        in_specs=in_specs,
        out_specs=out_spec,
        scratch_shapes=scratch,
        compiler_params=params(),
        cost_estimate=BRIEF,
        name="combine_quant" if quantized else "combine_float",
    )(*operands)


def to_pairs(part, groups):
    width = part.shape[1]
    low = lax.axis_index("dp") & 1
    part = part.reshape(groups // 2, 2, -1, width)
    kept = lax.dynamic_index_in_dim(part, low, 1, keepdims=False)
    sent = lax.dynamic_index_in_dim(part, 1 - low, 1, keepdims=False)
    came = lax.ppermute(sent, "dp", [(i, i ^ 1) for i in range(groups)])
    return (kept.astype(f32) + came.astype(f32)).astype(bf16)


def to_tokens(both, groups):
    pairs = groups // 2
    high = lax.axis_index("dp") >> 1
    total = lax.dynamic_index_in_dim(both, high, 0, keepdims=False).astype(f32)
    for k in range(1, pairs):
        block = lax.dynamic_index_in_dim(both, lax.rem(high + k, pairs), 0, keepdims=False)
        came = lax.ppermute(block, "dp", [(i, (i + 2 * k) % groups) for i in range(groups)])
        total = total + came.astype(f32)
    return total


def from_all(x, axis):
    copies = jnp.broadcast_to(x, (lax.axis_size(axis),) + x.shape)
    return lax.all_to_all(copies, axis, split_axis=0, concat_axis=0)


def on_device(tokens, expert_ids, route_weights, gate_weight, up_weight, down_weight):
    groups = lax.axis_size("dp")
    experts = gate_weight.shape[0]
    choices = expert_ids.shape[1]

    payload = jnp.concatenate([expert_ids.T.astype(f32), route_weights.T], axis=0)
    route = from_all(payload, "dp").reshape(-1, payload.shape[1])
    all_tokens = lax.all_gather(tokens, ("dp", "expert"), axis=0)
    all_tokens = all_tokens.reshape((groups, -1) + tokens.shape)

    local_peak = channel_peak(gate_weight, up_weight)
    weight_peak = from_all(local_peak.reshape(experts, -1).astype(bf16), "expert")
    weight_peak = jnp.max(weight_peak, axis=0).astype(f32)
    down_weight, local_peak = lax.optimization_barrier((down_weight, local_peak))
    levels, level_scale = down_quant(down_weight)

    first = (lax.axis_index("dp") * experts).astype(jnp.int32).reshape(1)
    hot, share = prep(first, route, experts, groups, choices)
    hot_t = jnp.swapaxes(hot, 1, 2)
    hot, levels = lax.optimization_barrier((hot, levels))
    rows, smooth = expert_rows(hot, all_tokens, weight_peak, experts, groups)

    hf, *scales = float_hidden(rows, gate_weight, up_weight, smooth)
    scales = tuple(scales)
    wide_f = lax.all_gather(hf, "expert", axis=0)

    half = experts // 2
    more = experts - half
    some = (3 * more) // 4
    operands = (gate_weight, up_weight, smooth, scales)
    hq = quant_hidden(rows, *operands, 0, half, half, 0)
    wide_q = [lax.all_gather(hq, "expert", axis=0)]
    wide_f, hq = lax.optimization_barrier((wide_f, hq))
    part_f = combine(hot_t, share, wide_f, down_weight, jnp.ones_like(level_scale), False)
    both_f = to_pairs(part_f, groups)
    rows, part_f = lax.optimization_barrier((rows, part_f))
    hq = quant_hidden(rows, *operands, half, some, more, 0) if some else None
    rows, both_f = lax.optimization_barrier((rows, both_f))
    out_f = to_tokens(both_f, groups)
    hq = quant_hidden(rows, *operands, half + some, more - some, more, some, hq)
    wide_q.append(lax.all_gather(hq, "expert", axis=0))
    share, hq = lax.optimization_barrier((share, hq))
    earlier = combine(hot_t, share, wide_q[0], levels, level_scale, True, last=False)
    earlier, out_f = lax.optimization_barrier((earlier, out_f))
    out_q = []
    for at in range(2):
        part_q = combine(
            hot_t, share, wide_q[1], levels, level_scale, True, half, at, 2, earlier=earlier
        )
        out_q.append(to_tokens(to_pairs(part_q, groups), groups).astype(bf16))
        earlier, part_q = lax.optimization_barrier((earlier, part_q))
    return jnp.concatenate(out_q, axis=1), out_f


def solution(mesh):
    in_specs = (
        P("dp", "expert"),
        P("dp", None),
        P("dp", None),
        P("dp", "expert", None),
        P("dp", "expert", None),
        P("dp", None, "expert"),
    )
    out_specs = (P("dp", "expert"), P("dp", "expert"))
    return jax.shard_map(
        on_device, mesh=mesh, in_specs=in_specs, out_specs=out_specs, check_vma=False
    )
```

profile of v0, /device:TPU:0, one launch (start us, length us, event | category | flops | bytes accessed | tf_op | source)
XLA Modules:
  0.0 313.1 jit_solution(2726869532527359001)
XLA Ops:
  7.2 0.7 all-gather.9.cloned.1.call-update
  7.9 0.7 convert_bitcast_fusion
  8.6 0.7 pad_maximum_fusion.1
  9.3 0.6 broadcast_in_dim.9
  9.9 7.3 %all-to-all-start = ((f32[8,16,128]{2,1,0:T(8,128)}), f32[8,16,128]{2,1,0:T(8,128)S(1)}, u32[]{:S(2)}, u32[]{:S(2)}) async-start(f32[8,16,128]{2,1,0:T(8,128)} %broadcast_in_dim.9), calls=%async_computation | async-start | bytes 131072 | tf_op jit(solution)/shard_map/all_to_all | solution.py:513
  17.2 17.1 %channel_peak.1 = f32[8,1,4096]{2,1,0:T(1,128)} custom-call(bf16[8,384,4096]{2,1,0:T(8,128)(2,1)} %gate_ref.9, bf16[8,384,4096]{2,1,0:T(8,128)(2,1)} %up_ref.9), custom_call_target="tpu_custom_call" | custom-call | flops 1 | bytes 1 | tf_op jit(solution)/shard_map/channel_peak/pallas_call | solution.py:145
  34.3 1.0 convert_element_type.104
  35.4 0.7 broadcast_in_dim.10
  36.2 3.4 %all-to-all-start.1 = ((bf16[4,8,4096]{2,1,0:T(8,128)(2,1)}), bf16[4,8,4096]{2,1,0:T(8,128)(2,1)S(1)}, u32[]{:S(2)}, u32[]{:S(2)}) async-start(bf16[4,8,4096]{2,1,0:T(8,128)(2,1)} %broadcast_in_dim.10), calls=%async_computation.1 | async-start | bytes 524288 | tf_op jit(solution)/shard_map/all_to_all | solution.py:513
  39.6 29.8 %down_levels.1 = (bf16[8,1536,1024]{2,1,0:T(8,128)(2,1)}, f32[8,1,1024]{2,1,0:T(1,128)}) custom-call(bf16[8,1536,1024]{2,1,0:T(8,128)(2,1)} %refs_2_), custom_call_target="tpu_custom_call" | custom-call | flops 1 | bytes 1 | tf_op jit(solution)/shard_map/down_levels/pallas_call | solution.py:184
  69.4 2.7 routing_tables.1
  72.1 0.7 convert_element_type.106.peak_ref
  72.8 21.1 %all-gather.9.cloned.1.call-done = bf16[4096,1024]{1,0:T(8,128)(2,1)} async-done(((bf16[128,1024]{1,0:T(8,128)(2,1)}), bf16[4096,1024]{1,0:T(8,128)(2,1)}) %all-gather.9.cloned.1.call-update) | async-done | bytes 8388624 | tf_op jit(solution)/shard_map/all_gather | solution.py:523
  93.9 12.6 %expert_rows.1 = (bf16[8,160,4096]{2,1,0:T(8,128)(2,1)}, f32[8,1,4096]{2,1,0:T(1,128)}) custom-call(bf16[2,640,512]{2,1,0:T(8,128)(2,1)} %get-tuple-element.28.hot_ref, bf16[8,4,128,1024]{3,2,1,0:T(8,128)(2,1)} %bitcast.69, f32[8,4096]{1,0:T(8,128)} %convert_element_type.106.peak_ref), custom_call_target="tpu_custom_call" | custom-call | tf_op jit(solution)/shard_map/expert_rows/pallas_call | solution.py:223
  106.4 39.9 %float_hidden.1 = (bf16[8,160,384]{2,1,0:T(8,128)(2,1)}, f32[8,768,128]{2,1,0:T(8,128)}, f32[8,768,128]{2,1,0:T(8,128)}, f32[8,160,128]{2,1,0:T(8,128)}, f32[8,160,128]{2,1,0:T(8,128)}) custom-call(bf16[8,160,4096]{2,1,0:T(8,128)(2,1)} %get-tuple-element.38.rows_ref, bf16[8,384,4096]{2,1,0:T(8,128)(2,1)} %gate_ref.9, bf16[8,384,4096]{2,1,0:T(8,128)(2,1)} %up_ref.9, ...), custom_call_target="tpu_custom_call" | custom-call | flops 1 | bytes 1 | tf_op jit(solution)/shard_map/float_hidden/pallas_call | solution.py:305
  146.5 26.7 %quant_hidden.3 = bf16[4,160,384]{2,1,0:T(8,128)(2,1)} custom-call(bf16[8,160,4096]{2,1,0:T(8,128)(2,1)} %get-tuple-element.38.rows_ref, bf16[8,384,4096]{2,1,0:T(8,128)(2,1)} %gate_ref.9, bf16[8,384,4096]{2,1,0:T(8,128)(2,1)} %up_ref.9, f32[8,1,4096]{2,1,0:T(1,128)} %get-tuple-element.30.smooth_ref, f32[8,768,128]{2,1,0:T(8,128)} %get-tuple-element.32.inverse_w, ...), custom_call_target="tpu_custom_call" | custom-call | flops 1 | bytes 1 | tf_op jit(solution)/shard_map/quant_hidden/pallas_call | solution.py:381
  173.2 0.2 all-gather.13.cloned.1.call-start
  173.5 1.4 copy.21
  174.9 3.2 %all-gather.11.cloned.1.call-done = bf16[32,160,384]{2,1,0:T(8,128)(2,1)} async-done(((bf16[8,160,384]{2,1,0:T(8,128)(2,1)}), bf16[32,160,384]{2,1,0:T(8,128)(2,1)}) %all-gather.11.cloned.1.call-update) | async-done | bytes 3932176 | tf_op jit(solution)/shard_map/all_gather | solution.py:540
  178.1 0.6 broadcast_in_dim.11.refs_3_
  178.8 16.6 %combine_float.1 = bf16[1024,1024]{1,0:T(8,128)(2,1)} custom-call(f32[8,160,1]{2,1,0:T(8,128)} %get-tuple-element.39.refs_0_, bf16[4,8,160,384]{3,2,1,0:T(8,128)(2,1)} %bitcast.76, bf16[8,1536,1024]{2,1,0:T(8,128)(2,1)} %refs_2_, f32[8,1,1024]{2,1,0:T(1,128)} %broadcast_in_dim.11.refs_3_, bf16[2,512,640]{2,1,0:T(8,128)(2,1)} %bitcast.64), custom_call_target="tpu_custom_call" | custom-call | flops 1 | bytes 1 | tf_op jit(solution)/shard_map/combine_float/pallas_call | solution.py:477
  195.4 1.3 dynamic-slice_bitcast_fusion
  196.7 1.6 collective-permute-start
  198.3 21.2 %quant_hidden.4.refs_0_ = bf16[4,160,384]{2,1,0:T(8,128)(2,1)} custom-call(bf16[8,160,4096]{2,1,0:T(8,128)(2,1)} %get-tuple-element.38.rows_ref, bf16[8,384,4096]{2,1,0:T(8,128)(2,1)} %gate_ref.9, bf16[8,384,4096]{2,1,0:T(8,128)(2,1)} %up_ref.9, f32[8,1,4096]{2,1,0:T(1,128)} %get-tuple-element.30.smooth_ref, f32[8,768,128]{2,1,0:T(8,128)} %get-tuple-element.32.inverse_w, ...), custom_call_target="tpu_custom_call" | custom-call | flops 1 | bytes 1 | tf_op jit(solution)/shard_map/quant_hidden/pallas_call | solution.py:381
  219.4 2.6 collective-permute-done
  222.1 0.4 fusion
  222.5 9.6 %quant_hidden.5 = bf16[4,160,384]{2,1,0:T(8,128)(2,1)} custom-call(bf16[8,160,4096]{2,1,0:T(8,128)(2,1)} %get-tuple-element.38.rows_ref, bf16[8,384,4096]{2,1,0:T(8,128)(2,1)} %gate_ref.9, bf16[8,384,4096]{2,1,0:T(8,128)(2,1)} %up_ref.9, f32[8,1,4096]{2,1,0:T(1,128)} %get-tuple-element.30.smooth_ref, ...), custom_call_target="tpu_custom_call", output_to_operand_aliasing={{}: (8, {})} | custom-call | flops 1 | bytes 1 | tf_op jit(solution)/shard_map/quant_hidden/pallas_call | solution.py:381
  232.3 1.6 collective-permute-start.1
  233.8 2.4 collective-permute-start.2
  236.2 1.5 collective-permute-start.3
  237.7 9.1 %combine_quant.3.refs_5_ = bf16[2,320,1024]{2,1,0:T(8,128)(2,1)} custom-call(f32[8,160,1]{2,1,0:T(8,128)} %get-tuple-element.39.refs_0_, bf16[4,4,160,384]{3,2,1,0:T(8,128)(2,1)} %bitcast.77, bf16[8,1536,1024]{2,1,0:T(8,128)(2,1)} %get-tuple-element.40.refs_2_, f32[8,1,1024]{2,1,0:T(1,128)} %get-tuple-element.41.refs_3_), custom_call_target="tpu_custom_call" | custom-call | flops 1 | bytes 1 | tf_op jit(solution)/shard_map/combine_quant/pallas_call | solution.py:477
  246.7 6.4 %collective-permute-done.2 = bf16[128,1024]{1,0:T(8,128)(2,1)S(1)} collective-permute-done((bf16[128,1024]{1,0:T(8,128)(2,1)S(1)}, bf16[128,1024]{1,0:T(8,128)(2,1)S(1)}, u32[]{:S(2)}, u32[]{:S(2)}) %collective-permute-start.2) | collective-permute-done | bytes 262176 | tf_op jit(solution)/shard_map/ppermute | solution.py:506
  253.1 1.0 fusion.4
  254.2 8.3 %combine_quant.4 = bf16[1024,512]{1,0:T(8,128)(2,1)} custom-call(f32[8,160,1]{2,1,0:T(8,128)} %get-tuple-element.39.refs_0_, bf16[4,4,160,384]{3,2,1,0:T(8,128)(2,1)} %bitcast.70, bf16[8,1536,1024]{2,1,0:T(8,128)(2,1)} %get-tuple-element.40.refs_2_, f32[8,1,1024]{2,1,0:T(1,128)} %get-tuple-element.41.refs_3_, bf16[2,512,640]{2,1,0:T(8,128)(2,1)} %bitcast.65, ...), custom_call_target="tpu_custom_call" | custom-call | flops 1 | bytes 1 | tf_op jit(solution)/shard_map/combine_quant/pallas_call | solution.py:477
  262.5 1.1 dynamic-slice_bitcast_fusion.2
  263.5 1.5 collective-permute-start.4
  265.1 8.3 %combine_quant.5 = bf16[1024,512]{1,0:T(8,128)(2,1)} custom-call(f32[8,160,1]{2,1,0:T(8,128)} %get-tuple-element.39.refs_0_, bf16[4,4,160,384]{3,2,1,0:T(8,128)(2,1)} %bitcast.71, bf16[8,1536,1024]{2,1,0:T(8,128)(2,1)} %get-tuple-element.40.refs_2_, f32[8,1,1024]{2,1,0:T(1,128)} %get-tuple-element.41.refs_3_, bf16[2,512,640]{2,1,0:T(8,128)(2,1)} %bitcast.66, ...), custom_call_target="tpu_custom_call" | custom-call | flops 1 | bytes 1 | tf_op jit(solution)/shard_map/combine_quant/pallas_call | solution.py:477
  273.4 1.2 dynamic-slice_bitcast_fusion.1
  274.6 0.6 collective-permute-start.8
  275.2 2.9 collective-permute-done.4
  278.3 5.8 %collective-permute-start.5 = (bf16[128,512]{1,0:T(8,128)(2,1)S(1)}, bf16[128,512]{1,0:T(8,128)(2,1)S(1)}, u32[]{:S(2)}, u32[]{:S(2)}) collective-permute-start(bf16[128,512]{1,0:T(8,128)(2,1)S(1)} %get-tuple-element.49), channel_id=1, source_target_pairs={{0,8},{4,12},{8,16},{12,20},{16,24},{20,28},{24,0},{28,4},{1,9},{5... | collective-permute-start | bytes 393224 | tf_op jit(solution)/shard_map/ppermute | solution.py:506
  284.2 2.3 collective-permute-start.7
  286.5 2.4 collective-permute-done.8
  289.1 4.8 %collective-permute-start.10 = (bf16[128,512]{1,0:T(8,128)(2,1)S(1)}, bf16[128,512]{1,0:T(8,128)(2,1)S(1)}, u32[]{:S(2)}, u32[]{:S(2)}) collective-permute-start(bf16[128,512]{1,0:T(8,128)(2,1)S(1)} %get-tuple-element.54), channel_id=1, source_target_pairs={{0,16},{4,20},{8,24},{12,28},{16,0},{20,4},{24,8},{28,12},{1,17},{... | collective-permute-start | bytes 393224 | tf_op jit(solution)/shard_map/ppermute | solution.py:506
  293.9 3.4 %collective-permute-start.11 = (bf16[128,512]{1,0:T(8,128)(2,1)S(1)}, bf16[128,512]{1,0:T(8,128)(2,1)S(1)}, u32[]{:S(2)}, u32[]{:S(2)}) collective-permute-start(bf16[128,512]{1,0:T(8,128)(2,1)S(1)} %get-tuple-element.53), channel_id=1, source_target_pairs={{0,24},{4,28},{8,0},{12,4},{16,8},{20,12},{24,16},{28,20},{1,25},{... | collective-permute-start | bytes 393224 | tf_op jit(solution)/shard_map/ppermute | solution.py:506
  297.4 3.2 %collective-permute-done.10 = bf16[128,512]{1,0:T(8,128)(2,1)S(1)} collective-permute-done((bf16[128,512]{1,0:T(8,128)(2,1)S(1)}, bf16[128,512]{1,0:T(8,128)(2,1)S(1)}, u32[]{:S(2)}, u32[]{:S(2)}) %collective-permute-start.10) | collective-permute-done | bytes 131104 | tf_op jit(solution)/shard_map/ppermute | solution.py:506
  300.7 5.0 %collective-permute-done.9 = bf16[128,512]{1,0:T(8,128)(2,1)S(1)} collective-permute-done((bf16[128,512]{1,0:T(8,128)(2,1)S(1)}, bf16[128,512]{1,0:T(8,128)(2,1)S(1)}, u32[]{:S(2)}, u32[]{:S(2)}) %collective-permute-start.9) | collective-permute-done | bytes 131104 | tf_op jit(solution)/shard_map/ppermute | solution.py:506
  305.8 0.7 pad_maximum_fusion
  (37 shorter events, 1.2 us)
Async XLA Ops:
  7.2 86.7 %all-gather.9.cloned.1.call-start = ((), (), s32[]{:S(2)}) async-start(), calls=%async_computation.2 | async-start | bytes 8650752 | tf_op jit(solution)/shard_map/all_gather | solution.py:523
  9.9 25.5 %all-to-all-start = ((f32[8,16,128]{2,1,0:T(8,128)}), f32[8,16,128]{2,1,0:T(8,128)S(1)}, u32[]{:S(2)}, u32[]{:S(2)}) async-start(f32[8,16,128]{2,1,0:T(8,128)} %broadcast_in_dim.9), calls=%async_computation | async-start | bytes 131072 | tf_op jit(solution)/shard_map/all_to_all | solution.py:513
  35.4 34.0 %copy-start.4 = (f32[8,16,128]{2,1,0:T(8,128)}, f32[8,16,128]{2,1,0:T(8,128)S(1)}, u32[]{:S(2)}) copy-start(f32[8,16,128]{2,1,0:T(8,128)S(1)} %all-to-all-done) | copy-start | bytes 196612
  36.2 35.9 %all-to-all-start.1 = ((bf16[4,8,4096]{2,1,0:T(8,128)(2,1)}), bf16[4,8,4096]{2,1,0:T(8,128)(2,1)S(1)}, u32[]{:S(2)}, u32[]{:S(2)}) async-start(bf16[4,8,4096]{2,1,0:T(8,128)(2,1)} %broadcast_in_dim.10), calls=%async_computation.1 | async-start | bytes 524288 | tf_op jit(solution)/shard_map/all_to_all | solution.py:513
  39.6 138.6 %all-gather.11.cloned.1.call-start = ((), (), s32[]{:S(2)}) async-start(), calls=%async_computation.3 | async-start | bytes 4915200 | tf_op jit(solution)/shard_map/all_gather | solution.py:540
  146.4 91.3 %all-gather.15.cloned.1.call-start = ((), (), s32[]{:S(2)}) async-start(), calls=%async_computation.5 | async-start | bytes 2457600 | tf_op jit(solution)/shard_map/all_gather | solution.py:547
  146.4 27.0 %copy-start.1 = (bf16[2,640,512]{2,1,0:T(8,128)(2,1)S(1)}, bf16[2,640,512]{2,1,0:T(8,128)(2,1)}, u32[]{:S(2)}) copy-start(bf16[2,640,512]{2,1,0:T(8,128)(2,1)} %get-tuple-element.28.hot_ref) | copy-start | bytes 3932164
  173.2 81.0 %all-gather.13.cloned.1.call-start = ((), (), s32[]{:S(2)}) async-start(), calls=%async_computation.4 | async-start | bytes 2457600 | tf_op jit(solution)/shard_map/all_gather | solution.py:556
  196.7 25.4 %collective-permute-start = (bf16[4,128,1024]{2,1,0:T(8,128)(2,1)S(1)}, bf16[4,128,1024]{2,1,0:T(8,128)(2,1)S(1)}, u32[]{:S(2)}, u32[]{:S(2)}) collective-permute-start(bf16[4,128,1024]{2,1,0:T(8,128)(2,1)S(1)} %dynamic-slice_bitcast_fusion), channel_id=1, source_target_pairs={{0,4},{4,0},{8,12},{12,8},{16,20},{20,16},{24,28},{28,24},{1,5},{5... | collective-permute-start | bytes 3145736 | tf_op jit(solution)/shard_map/ppermute | solution.py:496
  198.3 23.8 %copy-start = (bf16[1024,1024]{1,0:T(8,128)(2,1)S(1)}, bf16[1024,1024]{1,0:T(8,128)(2,1)}, u32[]{:S(2)}) copy-start(bf16[1024,1024]{1,0:T(8,128)(2,1)} %combine_float.1) | copy-start | bytes 6291460
  232.3 14.5 %collective-permute-start.1 = (bf16[128,1024]{1,0:T(8,128)(2,1)S(1)}, bf16[128,1024]{1,0:T(8,128)(2,1)S(1)}, u32[]{:S(2)}, u32[]{:S(2)}) collective-permute-start(bf16[128,1024]{1,0:T(8,128)(2,1)S(1)} %get-tuple-element.46), channel_id=1, source_target_pairs={{0,8},{4,12},{8,16},{12,20},{16,24},{20,28},{24,0},{28,4},{1,9},{5... | collective-permute-start | bytes 786440 | tf_op jit(solution)/shard_map/ppermute | solution.py:506
  233.8 19.3 %collective-permute-start.2 = (bf16[128,1024]{1,0:T(8,128)(2,1)S(1)}, bf16[128,1024]{1,0:T(8,128)(2,1)S(1)}, u32[]{:S(2)}, u32[]{:S(2)}) collective-permute-start(bf16[128,1024]{1,0:T(8,128)(2,1)S(1)} %get-tuple-element.48), channel_id=1, source_target_pairs={{0,16},{4,20},{8,24},{12,28},{16,0},{20,4},{24,8},{28,12},{1,17},{... | collective-permute-start | bytes 786440 | tf_op jit(solution)/shard_map/ppermute | solution.py:506
  236.2 16.9 %collective-permute-start.3 = (bf16[128,1024]{1,0:T(8,128)(2,1)S(1)}, bf16[128,1024]{1,0:T(8,128)(2,1)S(1)}, u32[]{:S(2)}, u32[]{:S(2)}) collective-permute-start(bf16[128,1024]{1,0:T(8,128)(2,1)S(1)} %get-tuple-element.47), channel_id=1, source_target_pairs={{0,24},{4,28},{8,0},{12,4},{16,8},{20,12},{24,16},{28,20},{1,25},{... | collective-permute-start | bytes 786440 | tf_op jit(solution)/shard_map/ppermute | solution.py:506
  263.5 14.6 %copy-start.3 = (bf16[1024,512]{1,0:T(8,128)(2,1)S(1)}, bf16[1024,512]{1,0:T(8,128)(2,1)}, u32[]{:S(2)}) copy-start(bf16[1024,512]{1,0:T(8,128)(2,1)} %combine_quant.4) | copy-start | bytes 3145732
  263.5 14.5 %collective-permute-start.4 = (bf16[4,128,512]{2,1,0:T(8,128)(2,1)S(1)}, bf16[4,128,512]{2,1,0:T(8,128)(2,1)S(1)}, u32[]{:S(2)}, u32[]{:S(2)}) collective-permute-start(bf16[4,128,512]{2,1,0:T(8,128)(2,1)S(1)} %dynamic-slice_bitcast_fusion.2), channel_id=1, source_target_pairs={{0,4},{4,0},{8,12},{12,8},{16,20},{20,16},{24,28},{28,24},{1,5},{5... | collective-permute-start | bytes 1572872 | tf_op jit(solution)/shard_map/ppermute | solution.py:496
  273.4 15.5 %copy-start.2 = (bf16[1024,512]{1,0:T(8,128)(2,1)S(1)}, bf16[1024,512]{1,0:T(8,128)(2,1)}, u32[]{:S(2)}) copy-start(bf16[1024,512]{1,0:T(8,128)(2,1)} %combine_quant.5) | copy-start | bytes 3145732
  274.6 14.3 %collective-permute-start.8 = (bf16[4,128,512]{2,1,0:T(8,128)(2,1)S(1)}, bf16[4,128,512]{2,1,0:T(8,128)(2,1)S(1)}, u32[]{:S(2)}, u32[]{:S(2)}) collective-permute-start(bf16[4,128,512]{2,1,0:T(8,128)(2,1)S(1)} %dynamic-slice_bitcast_fusion.1), channel_id=1, source_target_pairs={{0,4},{4,0},{8,12},{12,8},{16,20},{20,16},{24,28},{28,24},{1,5},{5... | collective-permute-start | bytes 1572872 | tf_op jit(solution)/shard_map/ppermute | solution.py:496
  278.3 19.0 %collective-permute-start.5 = (bf16[128,512]{1,0:T(8,128)(2,1)S(1)}, bf16[128,512]{1,0:T(8,128)(2,1)S(1)}, u32[]{:S(2)}, u32[]{:S(2)}) collective-permute-start(bf16[128,512]{1,0:T(8,128)(2,1)S(1)} %get-tuple-element.49), channel_id=1, source_target_pairs={{0,8},{4,12},{8,16},{12,20},{16,24},{20,28},{24,0},{28,4},{1,9},{5... | collective-permute-start | bytes 393224 | tf_op jit(solution)/shard_map/ppermute | solution.py:506
  284.1 13.2 %collective-permute-start.6 = (bf16[128,512]{1,0:T(8,128)(2,1)S(1)}, bf16[128,512]{1,0:T(8,128)(2,1)S(1)}, u32[]{:S(2)}, u32[]{:S(2)}) collective-permute-start(bf16[128,512]{1,0:T(8,128)(2,1)S(1)} %get-tuple-element.51), channel_id=1, source_target_pairs={{0,16},{4,20},{8,24},{12,28},{16,0},{20,4},{24,8},{28,12},{1,17},{... | collective-permute-start | bytes 393224 | tf_op jit(solution)/shard_map/ppermute | solution.py:506
  284.2 13.1 %collective-permute-start.7 = (bf16[128,512]{1,0:T(8,128)(2,1)S(1)}, bf16[128,512]{1,0:T(8,128)(2,1)S(1)}, u32[]{:S(2)}, u32[]{:S(2)}) collective-permute-start(bf16[128,512]{1,0:T(8,128)(2,1)S(1)} %get-tuple-element.50), channel_id=1, source_target_pairs={{0,24},{4,28},{8,0},{12,4},{16,8},{20,12},{24,16},{28,20},{1,25},{... | collective-permute-start | bytes 393224 | tf_op jit(solution)/shard_map/ppermute | solution.py:506
  289.1 11.5 %collective-permute-start.10 = (bf16[128,512]{1,0:T(8,128)(2,1)S(1)}, bf16[128,512]{1,0:T(8,128)(2,1)S(1)}, u32[]{:S(2)}, u32[]{:S(2)}) collective-permute-start(bf16[128,512]{1,0:T(8,128)(2,1)S(1)} %get-tuple-element.54), channel_id=1, source_target_pairs={{0,16},{4,20},{8,24},{12,28},{16,0},{20,4},{24,8},{28,12},{1,17},{... | collective-permute-start | bytes 393224 | tf_op jit(solution)/shard_map/ppermute | solution.py:506
  293.9 6.8 %collective-permute-start.11 = (bf16[128,512]{1,0:T(8,128)(2,1)S(1)}, bf16[128,512]{1,0:T(8,128)(2,1)S(1)}, u32[]{:S(2)}, u32[]{:S(2)}) collective-permute-start(bf16[128,512]{1,0:T(8,128)(2,1)S(1)} %get-tuple-element.53), channel_id=1, source_target_pairs={{0,24},{4,28},{8,0},{12,4},{16,8},{20,12},{24,16},{28,20},{1,25},{... | collective-permute-start | bytes 393224 | tf_op jit(solution)/shard_map/ppermute | solution.py:506
  297.3 8.4 %collective-permute-start.9 = (bf16[128,512]{1,0:T(8,128)(2,1)S(1)}, bf16[128,512]{1,0:T(8,128)(2,1)S(1)}, u32[]{:S(2)}, u32[]{:S(2)}) collective-permute-start(bf16[128,512]{1,0:T(8,128)(2,1)S(1)} %get-tuple-element.52), channel_id=1, source_target_pairs={{0,8},{4,12},{8,16},{12,20},{16,24},{20,28},{24,0},{28,4},{1,9},{5... | collective-permute-start | bytes 393224 | tf_op jit(solution)/shard_map/ppermute | solution.py:506
Sparse Core Ops, SparseCore 0:
  10.9 82.9 all-gather.8
  146.5 31.5 all-gather.10
  180.3 21.8 all-gather.14
  232.3 21.8 all-gather.12
where the time goes:
time: 314 us; the launch traced here: 313 us
  Pallas kernels  202 us (64%)
  waiting for transfers between devices  47.8 us (15%)
  starting transfers between devices  36.6 us (12%)
  between operations  13.9 us (4%)
  local copies, waits for them, and re-layouts  7.21 us (2%)
  other arithmetic  5.59 us (2%)
    pallas_call x3, Pallas kernels, quant_hidden(): pl.pallas_call(quant_kernel, grid=(amount,), out_shape=jax.ShapeDtypeStru...  57.6 us
    pallas_call x4, Pallas kernels, combine(): pl.pallas_call(functools.partial(combine_kernel, quantized, first, last),...  42.3 us
    pallas_call x1, Pallas kernels, float_hidden(): pl.pallas_call(float_kernel, grid=(experts,), out_shape=tuple((jax.ShapeD...  39.9 us
    pallas_call x1, Pallas kernels, down_quant(): pl.pallas_call(functools.partial(down_quant_kernel, hidden, block), grid=...  29.8 us
    ppermute x9, starting transfers between devices, to_tokens(): lax.ppermute(block, 'dp', [(i, (i + 2 * k) % groups) for i in range(group...  21.9 us
    all_gather x1, waiting for transfers between devices, on_device(): all_tokens = lax.all_gather(tokens, ('dp', 'expert'), axis=0)  21.1 us
    pallas_call x1, Pallas kernels, channel_peak(): pl.pallas_call(channel_peak_kernel, grid=(experts,), out_shape=jax.ShapeD...  17.1 us
    ppermute x9, waiting for transfers between devices, to_tokens(): lax.ppermute(block, 'dp', [(i, (i + 2 * k) % groups) for i in range(group...  14.7 us
  transfers between devices with their start and end apart: 18, of which 10 were waited for; matrix products, arithmetic and copies ran while one was open for 3% of the time, Pallas kernels for 45%

commit v1 on v0

--- a/solution.py
+++ b/solution.py
@@ -14,6 +14,7 @@
 VMEM = 56 * 1024 * 1024
 LANES = 128
 SLAB = 16
+SPACING_ONE = 192.0
 CHUNK = 1024
 BRIEF = pl.CostEstimate(flops=1, bytes_accessed=1, transcendentals=0)
 
@@ -33,9 +34,10 @@
 
 
 def level_bf16(v):
-    n = jnp.round(v)
-    r = (v - n).astype(bf16)
-    return n.astype(bf16) + fraction(r, FRACTION_BF16)
+    v = v.astype(bf16)
+    offset = jnp.asarray(SPACING_ONE, bf16)
+    n = (v + offset) - offset
+    return n + fraction(v - n, FRACTION_BF16)
 
 
 def level_mixed(v):
@@ -155,7 +157,7 @@
 
 
 def down_quant_kernel(rows, width, down_ref, level_ref, scale_ref):
-    step = 8 * SLAB
+    step = 32 * SLAB
 
     def peak(i, carry):
         base = pl.multiple_of(i * step, step)
@@ -258,7 +260,7 @@
     weights = ((gate_ref, 0), (up_ref, hidden))
 
     smooth = smooth_ref[0]
-    smooth_s[...] = jnp.broadcast_to(smooth, smooth_s.shape)
+    smooth_s[...] = jnp.broadcast_to(smooth, smooth_s.shape).astype(bf16)
     unsmooth_s[...] = jnp.broadcast_to(1.0 / smooth, unsmooth_s.shape)
     top_s[...] = jnp.zeros_like(top_s)
     top_r[...] = jnp.zeros_like(top_r)
@@ -272,7 +274,7 @@
         for ref, base in weights:
             acc[base : base + hidden, :] += dot_t(ref[0, :, cols], rows)
             for f in range(0, hidden, SLAB):
-                value = jnp.abs(ref[0, f : f + SLAB, cols]).astype(f32) * smooth_c
+                value = jnp.abs(ref[0, f : f + SLAB, cols]) * smooth_c
                 spot = slice(base + f, base + f + SLAB)
                 top_s[spot, :] = jnp.maximum(top_s[spot, :], fold_max(value))
         for r in range(0, count, SLAB):
@@ -288,7 +290,7 @@
         inverse_r[0, r : r + SLAB, :] = jnp.broadcast_to(LEVELS / top, (SLAB, LANES))
         scale_r[0, r : r + SLAB, :] = jnp.broadcast_to(top / LEVELS, (SLAB, LANES))
     for f in range(0, 2 * hidden, LANES):
-        top = jnp.max(top_s[f : f + LANES, :], axis=1, keepdims=True) + EPS
+        top = jnp.max(top_s[f : f + LANES, :].astype(f32), axis=1, keepdims=True) + EPS
         inverse_w[0, f : f + LANES, :] = jnp.broadcast_to(LEVELS / top, (LANES, LANES))
         scale_w[0, f : f + LANES, :] = jnp.broadcast_to(top / LEVELS, (LANES, LANES))
 
@@ -309,9 +311,9 @@
         in_specs=[spec(count, depth), spec(hidden, depth), spec(hidden, depth), spec(1, depth)],
         out_specs=tuple(spec(*s) for s in tails),
         scratch_shapes=[
+            pltpu.VMEM((SLAB, depth), bf16),
             pltpu.VMEM((SLAB, depth), f32),
-            pltpu.VMEM((SLAB, depth), f32),
-            pltpu.VMEM((2 * hidden, LANES), f32),
+            pltpu.VMEM((2 * hidden, LANES), bf16),
             pltpu.VMEM((count, LANES), f32),
             pltpu.VMEM((2 * hidden, count), f32),
         ],

time: 314 us -> 311 us (level)
  Pallas kernels: 202 us -> 193 us
  waiting for transfers between devices: 47.8 us -> 53.3 us
    pallas_call x3, Pallas kernels: 57.6 us -> 54.3 us  [quant_hidden(): pl.pallas_call(quant_kernel, grid=(amount,), out_shape=jax.ShapeDtypeStru...]
  transfers between devices with their start and end apart: 18 -> 18, of which waited for: 10 -> 10; matrix products, arithmetic and copies ran while one was open for 3% -> 4% of each run, Pallas kernels for 45% -> 44%
where the time goes in v1:
time: 311 us; the launch traced here: 310 us
  Pallas kernels  193 us (62%)
  waiting for transfers between devices  53.3 us (17%)
  starting transfers between devices  36.6 us (12%)
  between operations  13.9 us (4%)
  local copies, waits for them, and re-layouts  7.21 us (2%)
  other arithmetic  5.59 us (2%)
    pallas_call x3, Pallas kernels, quant_hidden(): pl.pallas_call(quant_kernel, grid=(amount,), out_shape=jax.ShapeDtypeStru...  54.3 us
    pallas_call x4, Pallas kernels, combine(): pl.pallas_call(functools.partial(combine_kernel, quantized, first, last),...  42.3 us
    pallas_call x1, Pallas kernels, float_hidden(): pl.pallas_call(float_kernel, grid=(experts,), out_shape=tuple((jax.ShapeD...  36.8 us
    pallas_call x1, Pallas kernels, down_quant(): pl.pallas_call(functools.partial(down_quant_kernel, hidden, block), grid=...  27.1 us
    all_gather x1, waiting for transfers between devices, on_device(): all_tokens = lax.all_gather(tokens, ('dp', 'expert'), axis=0)  23.8 us
    ppermute x9, starting transfers between devices, to_tokens(): lax.ppermute(block, 'dp', [(i, (i + 2 * k) % groups) for i in range(group...  21.9 us
    pallas_call x1, Pallas kernels, channel_peak(): pl.pallas_call(channel_peak_kernel, grid=(experts,), out_shape=jax.ShapeD...  17.1 us
    ppermute x9, waiting for transfers between devices, to_tokens(): lax.ppermute(block, 'dp', [(i, (i + 2 * k) % groups) for i in range(group...  14.7 us
  transfers between devices with their start and end apart: 18, of which 10 were waited for; matrix products, arithmetic and copies ran while one was open for 4% of the time, Pallas kernels for 44%

profile of v1, /device:TPU:0, one launch (start us, length us, event | category | flops | bytes accessed | tf_op | source)
XLA Modules:
  0.0 309.5 jit_solution(15145390935968575961)
XLA Ops:
  7.2 0.7 all-gather.9.cloned.1.call-update
  7.9 0.7 convert_bitcast_fusion
  8.6 0.7 pad_maximum_fusion.1
  9.3 0.6 broadcast_in_dim.9
  9.9 7.3 %all-to-all-start = ((f32[8,16,128]{2,1,0:T(8,128)}), f32[8,16,128]{2,1,0:T(8,128)S(1)}, u32[]{:S(2)}, u32[]{:S(2)}) async-start(f32[8,16,128]{2,1,0:T(8,128)} %broadcast_in_dim.9), calls=%async_computation | async-start | bytes 131072 | tf_op jit(solution)/shard_map/all_to_all | solution.py:515
  17.2 17.1 %channel_peak.1 = f32[8,1,4096]{2,1,0:T(1,128)} custom-call(bf16[8,384,4096]{2,1,0:T(8,128)(2,1)} %gate_ref.9, bf16[8,384,4096]{2,1,0:T(8,128)(2,1)} %up_ref.9), custom_call_target="tpu_custom_call" | custom-call | flops 1 | bytes 1 | tf_op jit(solution)/shard_map/channel_peak/pallas_call | solution.py:147
  34.3 1.0 convert_element_type.104
  35.4 0.7 broadcast_in_dim.10
  36.2 3.4 %all-to-all-start.1 = ((bf16[4,8,4096]{2,1,0:T(8,128)(2,1)}), bf16[4,8,4096]{2,1,0:T(8,128)(2,1)S(1)}, u32[]{:S(2)}, u32[]{:S(2)}) async-start(bf16[4,8,4096]{2,1,0:T(8,128)(2,1)} %broadcast_in_dim.10), calls=%async_computation.1 | async-start | bytes 524288 | tf_op jit(solution)/shard_map/all_to_all | solution.py:515
  39.6 27.1 %down_levels.1 = (bf16[8,1536,1024]{2,1,0:T(8,128)(2,1)}, f32[8,1,1024]{2,1,0:T(1,128)}) custom-call(bf16[8,1536,1024]{2,1,0:T(8,128)(2,1)} %refs_2_), custom_call_target="tpu_custom_call" | custom-call | flops 1 | bytes 1 | tf_op jit(solution)/shard_map/down_levels/pallas_call | solution.py:186
  66.7 2.7 routing_tables.1
  69.4 0.7 convert_element_type.106.peak_ref
  70.1 23.8 %all-gather.9.cloned.1.call-done = bf16[4096,1024]{1,0:T(8,128)(2,1)} async-done(((bf16[128,1024]{1,0:T(8,128)(2,1)}), bf16[4096,1024]{1,0:T(8,128)(2,1)}) %all-gather.9.cloned.1.call-update) | async-done | bytes 8388624 | tf_op jit(solution)/shard_map/all_gather | solution.py:525
  93.9 12.6 %expert_rows.1 = (bf16[8,160,4096]{2,1,0:T(8,128)(2,1)}, f32[8,1,4096]{2,1,0:T(1,128)}) custom-call(bf16[2,640,512]{2,1,0:T(8,128)(2,1)} %get-tuple-element.28.hot_ref, bf16[8,4,128,1024]{3,2,1,0:T(8,128)(2,1)} %bitcast.69, f32[8,4096]{1,0:T(8,128)} %convert_element_type.106.peak_ref), custom_call_target="tpu_custom_call" | custom-call | tf_op jit(solution)/shard_map/expert_rows/pallas_call | solution.py:225
  106.4 36.8 %float_hidden.1 = (bf16[8,160,384]{2,1,0:T(8,128)(2,1)}, f32[8,768,128]{2,1,0:T(8,128)}, f32[8,768,128]{2,1,0:T(8,128)}, f32[8,160,128]{2,1,0:T(8,128)}, f32[8,160,128]{2,1,0:T(8,128)}) custom-call(bf16[8,160,4096]{2,1,0:T(8,128)(2,1)} %get-tuple-element.38.rows_ref, bf16[8,384,4096]{2,1,0:T(8,128)(2,1)} %gate_ref.9, bf16[8,384,4096]{2,1,0:T(8,128)(2,1)} %up_ref.9, ...), custom_call_target="tpu_custom_call" | custom-call | flops 1 | bytes 1 | tf_op jit(solution)/shard_map/float_hidden/pallas_call | solution.py:307
  143.3 25.1 %quant_hidden.3 = bf16[4,160,384]{2,1,0:T(8,128)(2,1)} custom-call(bf16[8,160,4096]{2,1,0:T(8,128)(2,1)} %get-tuple-element.38.rows_ref, bf16[8,384,4096]{2,1,0:T(8,128)(2,1)} %gate_ref.9, bf16[8,384,4096]{2,1,0:T(8,128)(2,1)} %up_ref.9, f32[8,1,4096]{2,1,0:T(1,128)} %get-tuple-element.30.smooth_ref, f32[8,768,128]{2,1,0:T(8,128)} %get-tuple-element.32.inverse_w, ...), custom_call_target="tpu_custom_call" | custom-call | flops 1 | bytes 1 | tf_op jit(solution)/shard_map/quant_hidden/pallas_call | solution.py:383
  168.5 0.2 all-gather.13.cloned.1.call-start
  168.7 1.4 copy.21
  170.2 4.9 %all-gather.11.cloned.1.call-done = bf16[32,160,384]{2,1,0:T(8,128)(2,1)} async-done(((bf16[8,160,384]{2,1,0:T(8,128)(2,1)}), bf16[32,160,384]{2,1,0:T(8,128)(2,1)}) %all-gather.11.cloned.1.call-update) | async-done | bytes 3932176 | tf_op jit(solution)/shard_map/all_gather | solution.py:542
  175.0 0.6 broadcast_in_dim.11.refs_3_
  175.6 16.6 %combine_float.1 = bf16[1024,1024]{1,0:T(8,128)(2,1)} custom-call(f32[8,160,1]{2,1,0:T(8,128)} %get-tuple-element.39.refs_0_, bf16[4,8,160,384]{3,2,1,0:T(8,128)(2,1)} %bitcast.76, bf16[8,1536,1024]{2,1,0:T(8,128)(2,1)} %refs_2_, f32[8,1,1024]{2,1,0:T(1,128)} %broadcast_in_dim.11.refs_3_, bf16[2,512,640]{2,1,0:T(8,128)(2,1)} %bitcast.64), custom_call_target="tpu_custom_call" | custom-call | flops 1 | bytes 1 | tf_op jit(solution)/shard_map/combine_float/pallas_call | solution.py:479
  192.3 1.3 dynamic-slice_bitcast_fusion
  193.6 1.6 collective-permute-start
  195.1 20.0 %quant_hidden.4.refs_0_ = bf16[4,160,384]{2,1,0:T(8,128)(2,1)} custom-call(bf16[8,160,4096]{2,1,0:T(8,128)(2,1)} %get-tuple-element.38.rows_ref, bf16[8,384,4096]{2,1,0:T(8,128)(2,1)} %gate_ref.9, bf16[8,384,4096]{2,1,0:T(8,128)(2,1)} %up_ref.9, f32[8,1,4096]{2,1,0:T(1,128)} %get-tuple-element.30.smooth_ref, f32[8,768,128]{2,1,0:T(8,128)} %get-tuple-element.32.inverse_w, ...), custom_call_target="tpu_custom_call" | custom-call | flops 1 | bytes 1 | tf_op jit(solution)/shard_map/quant_hidden/pallas_call | solution.py:383
  215.1 3.9 %collective-permute-done = bf16[4,128,1024]{2,1,0:T(8,128)(2,1)S(1)} collective-permute-done((bf16[4,128,1024]{2,1,0:T(8,128)(2,1)S(1)}, bf16[4,128,1024]{2,1,0:T(8,128)(2,1)S(1)}, u32[]{:S(2)}, u32[]{:S(2)}) %collective-permute-start) | collective-permute-done | bytes 1048608 | tf_op jit(solution)/shard_map/ppermute | solution.py:498
  219.0 0.4 fusion
  219.4 9.2 %quant_hidden.5 = bf16[4,160,384]{2,1,0:T(8,128)(2,1)} custom-call(bf16[8,160,4096]{2,1,0:T(8,128)(2,1)} %get-tuple-element.38.rows_ref, bf16[8,384,4096]{2,1,0:T(8,128)(2,1)} %gate_ref.9, bf16[8,384,4096]{2,1,0:T(8,128)(2,1)} %up_ref.9, f32[8,1,4096]{2,1,0:T(1,128)} %get-tuple-element.30.smooth_ref, ...), custom_call_target="tpu_custom_call", output_to_operand_aliasing={{}: (8, {})} | custom-call | flops 1 | bytes 1 | tf_op jit(solution)/shard_map/quant_hidden/pallas_call | solution.py:383
  228.7 1.6 collective-permute-start.1
  230.3 2.4 collective-permute-start.2
  232.7 1.4 collective-permute-start.3
  234.1 9.1 %combine_quant.3.refs_5_ = bf16[2,320,1024]{2,1,0:T(8,128)(2,1)} custom-call(f32[8,160,1]{2,1,0:T(8,128)} %get-tuple-element.39.refs_0_, bf16[4,4,160,384]{3,2,1,0:T(8,128)(2,1)} %bitcast.77, bf16[8,1536,1024]{2,1,0:T(8,128)(2,1)} %get-tuple-element.40.refs_2_, f32[8,1,1024]{2,1,0:T(1,128)} %get-tuple-element.41.refs_3_), custom_call_target="tpu_custom_call" | custom-call | flops 1 | bytes 1 | tf_op jit(solution)/shard_map/combine_quant/pallas_call | solution.py:479
  243.2 6.4 %collective-permute-done.2 = bf16[128,1024]{1,0:T(8,128)(2,1)S(1)} collective-permute-done((bf16[128,1024]{1,0:T(8,128)(2,1)S(1)}, bf16[128,1024]{1,0:T(8,128)(2,1)S(1)}, u32[]{:S(2)}, u32[]{:S(2)}) %collective-permute-start.2) | collective-permute-done | bytes 262176 | tf_op jit(solution)/shard_map/ppermute | solution.py:508
  249.6 1.0 fusion.4
  250.7 8.2 %combine_quant.4 = bf16[1024,512]{1,0:T(8,128)(2,1)} custom-call(f32[8,160,1]{2,1,0:T(8,128)} %get-tuple-element.39.refs_0_, bf16[4,4,160,384]{3,2,1,0:T(8,128)(2,1)} %bitcast.70, bf16[8,1536,1024]{2,1,0:T(8,128)(2,1)} %get-tuple-element.40.refs_2_, f32[8,1,1024]{2,1,0:T(1,128)} %get-tuple-element.41.refs_3_, bf16[2,512,640]{2,1,0:T(8,128)(2,1)} %bitcast.65, ...), custom_call_target="tpu_custom_call" | custom-call | flops 1 | bytes 1 | tf_op jit(solution)/shard_map/combine_quant/pallas_call | solution.py:479
  258.9 1.1 dynamic-slice_bitcast_fusion.2
  260.0 1.5 collective-permute-start.4
  261.5 8.3 %combine_quant.5 = bf16[1024,512]{1,0:T(8,128)(2,1)} custom-call(f32[8,160,1]{2,1,0:T(8,128)} %get-tuple-element.39.refs_0_, bf16[4,4,160,384]{3,2,1,0:T(8,128)(2,1)} %bitcast.71, bf16[8,1536,1024]{2,1,0:T(8,128)(2,1)} %get-tuple-element.40.refs_2_, f32[8,1,1024]{2,1,0:T(1,128)} %get-tuple-element.41.refs_3_, bf16[2,512,640]{2,1,0:T(8,128)(2,1)} %bitcast.66, ...), custom_call_target="tpu_custom_call" | custom-call | flops 1 | bytes 1 | tf_op jit(solution)/shard_map/combine_quant/pallas_call | solution.py:479
  269.9 1.2 dynamic-slice_bitcast_fusion.1
  271.0 0.6 collective-permute-start.8
  271.7 2.9 collective-permute-done.4
  274.7 5.8 %collective-permute-start.5 = (bf16[128,512]{1,0:T(8,128)(2,1)S(1)}, bf16[128,512]{1,0:T(8,128)(2,1)S(1)}, u32[]{:S(2)}, u32[]{:S(2)}) collective-permute-start(bf16[128,512]{1,0:T(8,128)(2,1)S(1)} %get-tuple-element.49), channel_id=1, source_target_pairs={{0,8},{4,12},{8,16},{12,20},{16,24},{20,28},{24,0},{28,4},{1,9},{5... | collective-permute-start | bytes 393224 | tf_op jit(solution)/shard_map/ppermute | solution.py:508
  280.6 2.4 collective-permute-start.7
  283.0 2.4 collective-permute-done.8
  285.6 4.8 %collective-permute-start.10 = (bf16[128,512]{1,0:T(8,128)(2,1)S(1)}, bf16[128,512]{1,0:T(8,128)(2,1)S(1)}, u32[]{:S(2)}, u32[]{:S(2)}) collective-permute-start(bf16[128,512]{1,0:T(8,128)(2,1)S(1)} %get-tuple-element.54), channel_id=1, source_target_pairs={{0,16},{4,20},{8,24},{12,28},{16,0},{20,4},{24,8},{28,12},{1,17},{... | collective-permute-start | bytes 393224 | tf_op jit(solution)/shard_map/ppermute | solution.py:508
  290.4 3.4 %collective-permute-start.11 = (bf16[128,512]{1,0:T(8,128)(2,1)S(1)}, bf16[128,512]{1,0:T(8,128)(2,1)S(1)}, u32[]{:S(2)}, u32[]{:S(2)}) collective-permute-start(bf16[128,512]{1,0:T(8,128)(2,1)S(1)} %get-tuple-element.53), channel_id=1, source_target_pairs={{0,24},{4,28},{8,0},{12,4},{16,8},{20,12},{24,16},{28,20},{1,25},{... | collective-permute-start | bytes 393224 | tf_op jit(solution)/shard_map/ppermute | solution.py:508
  293.9 3.2 %collective-permute-done.10 = bf16[128,512]{1,0:T(8,128)(2,1)S(1)} collective-permute-done((bf16[128,512]{1,0:T(8,128)(2,1)S(1)}, bf16[128,512]{1,0:T(8,128)(2,1)S(1)}, u32[]{:S(2)}, u32[]{:S(2)}) %collective-permute-start.10) | collective-permute-done | bytes 131104 | tf_op jit(solution)/shard_map/ppermute | solution.py:508
  297.1 5.0 %collective-permute-done.9 = bf16[128,512]{1,0:T(8,128)(2,1)S(1)} collective-permute-done((bf16[128,512]{1,0:T(8,128)(2,1)S(1)}, bf16[128,512]{1,0:T(8,128)(2,1)S(1)}, u32[]{:S(2)}, u32[]{:S(2)}) %collective-permute-start.9) | collective-permute-done | bytes 131104 | tf_op jit(solution)/shard_map/ppermute | solution.py:508
  302.3 0.7 pad_maximum_fusion
  (37 shorter events, 1.1 us)
Async XLA Ops:
  7.2 86.7 %all-gather.9.cloned.1.call-start = ((), (), s32[]{:S(2)}) async-start(), calls=%async_computation.2 | async-start | bytes 8650752 | tf_op jit(solution)/shard_map/all_gather | solution.py:525
  9.9 25.5 %all-to-all-start = ((f32[8,16,128]{2,1,0:T(8,128)}), f32[8,16,128]{2,1,0:T(8,128)S(1)}, u32[]{:S(2)}, u32[]{:S(2)}) async-start(f32[8,16,128]{2,1,0:T(8,128)} %broadcast_in_dim.9), calls=%async_computation | async-start | bytes 131072 | tf_op jit(solution)/shard_map/all_to_all | solution.py:515
  35.4 31.3 %copy-start.4 = (f32[8,16,128]{2,1,0:T(8,128)}, f32[8,16,128]{2,1,0:T(8,128)S(1)}, u32[]{:S(2)}) copy-start(f32[8,16,128]{2,1,0:T(8,128)S(1)} %all-to-all-done) | copy-start | bytes 196612
  36.2 33.2 %all-to-all-start.1 = ((bf16[4,8,4096]{2,1,0:T(8,128)(2,1)}), bf16[4,8,4096]{2,1,0:T(8,128)(2,1)S(1)}, u32[]{:S(2)}, u32[]{:S(2)}) async-start(bf16[4,8,4096]{2,1,0:T(8,128)(2,1)} %broadcast_in_dim.10), calls=%async_computation.1 | async-start | bytes 524288 | tf_op jit(solution)/shard_map/all_to_all | solution.py:515
  39.6 135.4 %all-gather.11.cloned.1.call-start = ((), (), s32[]{:S(2)}) async-start(), calls=%async_computation.3 | async-start | bytes 4915200 | tf_op jit(solution)/shard_map/all_gather | solution.py:542
  143.3 90.9 %all-gather.15.cloned.1.call-start = ((), (), s32[]{:S(2)}) async-start(), calls=%async_computation.5 | async-start | bytes 2457600 | tf_op jit(solution)/shard_map/all_gather | solution.py:549
  143.3 25.4 %copy-start.1 = (bf16[2,640,512]{2,1,0:T(8,128)(2,1)S(1)}, bf16[2,640,512]{2,1,0:T(8,128)(2,1)}, u32[]{:S(2)}) copy-start(bf16[2,640,512]{2,1,0:T(8,128)(2,1)} %get-tuple-element.28.hot_ref) | copy-start | bytes 3932164
  168.5 82.2 %all-gather.13.cloned.1.call-start = ((), (), s32[]{:S(2)}) async-start(), calls=%async_computation.4 | async-start | bytes 2457600 | tf_op jit(solution)/shard_map/all_gather | solution.py:558
  193.6 25.4 %collective-permute-start = (bf16[4,128,1024]{2,1,0:T(8,128)(2,1)S(1)}, bf16[4,128,1024]{2,1,0:T(8,128)(2,1)S(1)}, u32[]{:S(2)}, u32[]{:S(2)}) collective-permute-start(bf16[4,128,1024]{2,1,0:T(8,128)(2,1)S(1)} %dynamic-slice_bitcast_fusion), channel_id=1, source_target_pairs={{0,4},{4,0},{8,12},{12,8},{16,20},{20,16},{24,28},{28,24},{1,5},{5... | collective-permute-start | bytes 3145736 | tf_op jit(solution)/shard_map/ppermute | solution.py:498
  195.1 23.8 %copy-start = (bf16[1024,1024]{1,0:T(8,128)(2,1)S(1)}, bf16[1024,1024]{1,0:T(8,128)(2,1)}, u32[]{:S(2)}) copy-start(bf16[1024,1024]{1,0:T(8,128)(2,1)} %combine_float.1) | copy-start | bytes 6291460
  228.7 14.5 %collective-permute-start.1 = (bf16[128,1024]{1,0:T(8,128)(2,1)S(1)}, bf16[128,1024]{1,0:T(8,128)(2,1)S(1)}, u32[]{:S(2)}, u32[]{:S(2)}) collective-permute-start(bf16[128,1024]{1,0:T(8,128)(2,1)S(1)} %get-tuple-element.46), channel_id=1, source_target_pairs={{0,8},{4,12},{8,16},{12,20},{16,24},{20,28},{24,0},{28,4},{1,9},{5... | collective-permute-start | bytes 786440 | tf_op jit(solution)/shard_map/ppermute | solution.py:508
  230.3 19.3 %collective-permute-start.2 = (bf16[128,1024]{1,0:T(8,128)(2,1)S(1)}, bf16[128,1024]{1,0:T(8,128)(2,1)S(1)}, u32[]{:S(2)}, u32[]{:S(2)}) collective-permute-start(bf16[128,1024]{1,0:T(8,128)(2,1)S(1)} %get-tuple-element.48), channel_id=1, source_target_pairs={{0,16},{4,20},{8,24},{12,28},{16,0},{20,4},{24,8},{28,12},{1,17},{... | collective-permute-start | bytes 786440 | tf_op jit(solution)/shard_map/ppermute | solution.py:508
  232.7 16.9 %collective-permute-start.3 = (bf16[128,1024]{1,0:T(8,128)(2,1)S(1)}, bf16[128,1024]{1,0:T(8,128)(2,1)S(1)}, u32[]{:S(2)}, u32[]{:S(2)}) collective-permute-start(bf16[128,1024]{1,0:T(8,128)(2,1)S(1)} %get-tuple-element.47), channel_id=1, source_target_pairs={{0,24},{4,28},{8,0},{12,4},{16,8},{20,12},{24,16},{28,20},{1,25},{... | collective-permute-start | bytes 786440 | tf_op jit(solution)/shard_map/ppermute | solution.py:508
  260.0 14.6 %copy-start.3 = (bf16[1024,512]{1,0:T(8,128)(2,1)S(1)}, bf16[1024,512]{1,0:T(8,128)(2,1)}, u32[]{:S(2)}) copy-start(bf16[1024,512]{1,0:T(8,128)(2,1)} %combine_quant.4) | copy-start | bytes 3145732
  260.0 14.5 %collective-permute-start.4 = (bf16[4,128,512]{2,1,0:T(8,128)(2,1)S(1)}, bf16[4,128,512]{2,1,0:T(8,128)(2,1)S(1)}, u32[]{:S(2)}, u32[]{:S(2)}) collective-permute-start(bf16[4,128,512]{2,1,0:T(8,128)(2,1)S(1)} %dynamic-slice_bitcast_fusion.2), channel_id=1, source_target_pairs={{0,4},{4,0},{8,12},{12,8},{16,20},{20,16},{24,28},{28,24},{1,5},{5... | collective-permute-start | bytes 1572872 | tf_op jit(solution)/shard_map/ppermute | solution.py:498
  269.9 15.5 %copy-start.2 = (bf16[1024,512]{1,0:T(8,128)(2,1)S(1)}, bf16[1024,512]{1,0:T(8,128)(2,1)}, u32[]{:S(2)}) copy-start(bf16[1024,512]{1,0:T(8,128)(2,1)} %combine_quant.5) | copy-start | bytes 3145732
  271.0 14.3 %collective-permute-start.8 = (bf16[4,128,512]{2,1,0:T(8,128)(2,1)S(1)}, bf16[4,128,512]{2,1,0:T(8,128)(2,1)S(1)}, u32[]{:S(2)}, u32[]{:S(2)}) collective-permute-start(bf16[4,128,512]{2,1,0:T(8,128)(2,1)S(1)} %dynamic-slice_bitcast_fusion.1), channel_id=1, source_target_pairs={{0,4},{4,0},{8,12},{12,8},{16,20},{20,16},{24,28},{28,24},{1,5},{5... | collective-permute-start | bytes 1572872 | tf_op jit(solution)/shard_map/ppermute | solution.py:498
  274.7 19.0 %collective-permute-start.5 = (bf16[128,512]{1,0:T(8,128)(2,1)S(1)}, bf16[128,512]{1,0:T(8,128)(2,1)S(1)}, u32[]{:S(2)}, u32[]{:S(2)}) collective-permute-start(bf16[128,512]{1,0:T(8,128)(2,1)S(1)} %get-tuple-element.49), channel_id=1, source_target_pairs={{0,8},{4,12},{8,16},{12,20},{16,24},{20,28},{24,0},{28,4},{1,9},{5... | collective-permute-start | bytes 393224 | tf_op jit(solution)/shard_map/ppermute | solution.py:508
  280.6 13.2 %collective-permute-start.6 = (bf16[128,512]{1,0:T(8,128)(2,1)S(1)}, bf16[128,512]{1,0:T(8,128)(2,1)S(1)}, u32[]{:S(2)}, u32[]{:S(2)}) collective-permute-start(bf16[128,512]{1,0:T(8,128)(2,1)S(1)} %get-tuple-element.51), channel_id=1, source_target_pairs={{0,16},{4,20},{8,24},{12,28},{16,0},{20,4},{24,8},{28,12},{1,17},{... | collective-permute-start | bytes 393224 | tf_op jit(solution)/shard_map/ppermute | solution.py:508
  280.6 13.2 %collective-permute-start.7 = (bf16[128,512]{1,0:T(8,128)(2,1)S(1)}, bf16[128,512]{1,0:T(8,128)(2,1)S(1)}, u32[]{:S(2)}, u32[]{:S(2)}) collective-permute-start(bf16[128,512]{1,0:T(8,128)(2,1)S(1)} %get-tuple-element.50), channel_id=1, source_target_pairs={{0,24},{4,28},{8,0},{12,4},{16,8},{20,12},{24,16},{28,20},{1,25},{... | collective-permute-start | bytes 393224 | tf_op jit(solution)/shard_map/ppermute | solution.py:508
  285.6 11.5 %collective-permute-start.10 = (bf16[128,512]{1,0:T(8,128)(2,1)S(1)}, bf16[128,512]{1,0:T(8,128)(2,1)S(1)}, u32[]{:S(2)}, u32[]{:S(2)}) collective-permute-start(bf16[128,512]{1,0:T(8,128)(2,1)S(1)} %get-tuple-element.54), channel_id=1, source_target_pairs={{0,16},{4,20},{8,24},{12,28},{16,0},{20,4},{24,8},{28,12},{1,17},{... | collective-permute-start | bytes 393224 | tf_op jit(solution)/shard_map/ppermute | solution.py:508
  290.4 6.8 %collective-permute-start.11 = (bf16[128,512]{1,0:T(8,128)(2,1)S(1)}, bf16[128,512]{1,0:T(8,128)(2,1)S(1)}, u32[]{:S(2)}, u32[]{:S(2)}) collective-permute-start(bf16[128,512]{1,0:T(8,128)(2,1)S(1)} %get-tuple-element.53), channel_id=1, source_target_pairs={{0,24},{4,28},{8,0},{12,4},{16,8},{20,12},{24,16},{28,20},{1,25},{... | collective-permute-start | bytes 393224 | tf_op jit(solution)/shard_map/ppermute | solution.py:508
  293.8 8.4 %collective-permute-start.9 = (bf16[128,512]{1,0:T(8,128)(2,1)S(1)}, bf16[128,512]{1,0:T(8,128)(2,1)S(1)}, u32[]{:S(2)}, u32[]{:S(2)}) collective-permute-start(bf16[128,512]{1,0:T(8,128)(2,1)S(1)} %get-tuple-element.52), channel_id=1, source_target_pairs={{0,8},{4,12},{8,16},{12,20},{16,24},{20,28},{24,0},{28,4},{1,9},{5... | collective-permute-start | bytes 393224 | tf_op jit(solution)/shard_map/ppermute | solution.py:508
Sparse Core Ops, SparseCore 0:
  10.9 82.9 all-gather.8
  143.4 31.5 all-gather.10
  177.2 21.8 all-gather.14
  228.8 21.8 all-gather.12
